TPU v7x, 256 devices: a whole 4x4x8 slice. The times are simulated.
256 devices in a mesh: gx: 16 (over z_hi, y), gy: 4 (over z_lo, core), gz: 4 (over x).
Axes of the slice: x: 4, y: 4, z: 8 (z_hi: 4, z_lo: 2; z = z_hi * 2 + z_lo), core: 2. Of those that a mesh axis runs over, the one named last changes fastest.
Arguments:
- material_fraction: float32 [256, 256, 1024], P('gx', ('gy', 'gz')), may hold values from 0 to 1, as said below
- voxel_markers: int32 [256, 256, 1024], P('gx', 'gy', 'gz'), may hold values from 0 to 2, as said below
- pressure_drive: float32 [256, 256, 1024], P('gx', 'gy', 'gz'), may hold values from 0.5 to 4
- warmth_supply: float32 [256, 256, 1024], P('gx', 'gy', 'gz'), may hold values from 0.5 to 4
- prior_velocity: float32 [256, 256, 1024], P('gx', 'gy', 'gz'), may hold values from 0 to 1
- prior_warmth_level: float32 [256, 256, 1024], P('gx', 'gy', 'gz'), may hold values from 0 to 2
Outputs:
- speed_next: float32 [256, 256, 1024], P('gx', 'gy', 'gz')
- temperature_next: float32 [256, 256, 1024], P('gx', 'gy', 'gz')
- objective_derivative: float32 [256, 256, 1024], P('gx', ('gy', 'gz'))
Inputs may be any that keep to these rules, and one draw needn't show every extreme that they name: `voxel_markers`: 0 marks a design cell, 1 an inlet cell, 2 a wall cell. `material_fraction`: a design density for every cell.
All inputs are finite; a program needn't handle non-finite values.
Results may differ from a plain program's by a relative error of at most 0.00002.
Values sent between devices are 32-bit elements; how exact they have to be, the bound alone decides.
A program may use at most 128 MiB of HBM per device.

v0:
```python
import functools
import math

import jax
import jax.numpy as jnp
from jax import lax
from jax.experimental import pallas as pl
from jax.experimental.pallas import tpu as pltpu
from jax.sharding import PartitionSpec as P

MESH = pl.DeviceIdType.MESH
F32 = jnp.float32

TANH2 = math.tanh(2.0)
SCALE = 1.0 / 81.0**3


def tri_lanes(x):
    n = x.shape[1]
    a = x + pltpu.roll(x, 1, 1)
    a = a + pltpu.roll(a, 2, 1)
    a = a + pltpu.roll(a, 4, 1)
    a = a + pltpu.roll(x, 8, 1)
    b = a + pltpu.roll(a, n - 1, 1)
    b = b + pltpu.roll(b, n - 2, 1)
    b = b + pltpu.roll(b, n - 4, 1)
    return b + pltpu.roll(a, n - 8, 1)


def tri_rows(x):
    n = x.shape[0]
    a = x + pltpu.roll(x, 1, 0)
    a = a + pltpu.roll(a, 2, 0)
    a = a + pltpu.roll(a, 4, 0)
    a = a + pltpu.roll(x, 8, 0)
    b = a + pltpu.roll(a, 1, 0)
    b = b + pltpu.roll(b, 2, 0)
    b = b + pltpu.roll(b, 4, 0)
    b = b + pltpu.roll(a, 8, 0)
    return b[16:]


def box_lead(x):
    a = x[1:] + x[:-1]
    a = a[2:] + a[:-2]
    a = a[4:] + a[:-4]
    return a[1:] + x[: x.shape[0] - 8]


def tri_lead(x):
    return box_lead(box_lead(x))


class Exchange:
    def __init__(self, axis, low, high, land_low, land_high, sems):
        self.axis, self.low_src, self.high_src = axis, low, high
        self.land_low, self.land_high, self.sems = land_low, land_high, sems
        self.at, self.count = lax.axis_index(axis), lax.axis_size(axis)

    def low(self):
        return pltpu.make_async_remote_copy(
            src_ref=self.low_src, dst_ref=self.land_high, send_sem=self.sems[0], recv_sem=self.sems[1],
            device_id={self.axis: self.at - 1}, device_id_type=MESH)

    def high(self):
        return pltpu.make_async_remote_copy(
            src_ref=self.high_src, dst_ref=self.land_low, send_sem=self.sems[2], recv_sem=self.sems[3],
            device_id={self.axis: self.at + 1}, device_id_type=MESH)

    def has_low(self):
        return self.at > 0

    def has_high(self):
        return self.at < self.count - 1

    def start(self):
        @pl.when(self.has_low())
        def _():
            self.low().start()

        @pl.when(self.has_high())
        def _():
            self.high().start()

    def wait(self):
        @pl.when(self.has_low())
        def _():
            self.high().wait_recv()

        @pl.when(self.has_high())
        def _():
            self.low().wait_recv()

    def finish(self):
        @pl.when(self.has_low())
        def _():
            self.low().wait_send()

        @pl.when(self.has_high())
        def _():
            self.high().wait_send()

    def clear(self):
        @pl.when(self.at == 0)
        def _():
            self.land_low[...] = jnp.zeros(self.land_low.shape, F32)

        @pl.when(self.at == self.count - 1)
        def _():
            self.land_high[...] = jnp.zeros(self.land_high.shape, F32)


def kernel(mat_h, mark_h, press_h, warm_h, vel_h, temp_h, speed_o, temper_o, deriv_o,
           mat, mark, press, warm, st0, st1, st2, rinv, cond, gain, slope,
           zs, yl1, yh1, ds, q1, q2, us, yl2, yh2, ws, slab, outs,
           lx_lo, lx_hi, ys, yl, zsnd, zl,
           in_sem, out_sem, y1_sem, y2_sem, g1_sem, g2_sem, a1_sem, a2_sem, x_sem, r_sem, c_sem):
    gx, gy, gz = lax.axis_index("gx"), lax.axis_index("gy"), lax.axis_index("gz")
    nx, ny, nz = lax.axis_size("gx"), lax.axis_size("gy"), lax.axis_size("gz")
    lead, rows, cols = st0.shape[1:]
    thin = rows // nz

    loads = [pltpu.make_async_copy(src, dst, in_sem.at[k]) for k, (src, dst) in enumerate(
        [(mat_h, mat), (vel_h, st0.at[0]), (temp_h, st0.at[1]), (press_h, press), (warm_h, warm), (mark_h, mark)])]
    for load in loads:
        load.start()

    barrier = pltpu.get_barrier_semaphore()
    for axis, at, count in (("gx", gx, nx), ("gy", gy, ny)):
        @pl.when(at > 0)
        def _():
            pl.semaphore_signal(barrier, inc=1, device_id={axis: at - 1}, device_id_type=MESH)

        @pl.when(at < count - 1)
        def _():
            pl.semaphore_signal(barrier, inc=1, device_id={axis: at + 1}, device_id_type=MESH)
    for hop in range(1, nz):
        pl.semaphore_signal(barrier, inc=1, device_id={"gz": lax.rem(gz + hop, nz)}, device_id_type=MESH)

    y1 = [Exchange("gx", zs.at[c, 0:8], zs.at[c, lead - 8:lead], yl1.at[c], yh1.at[c],
                   [y1_sem.at[c, k] for k in range(4)]) for c in range(nz)]
    y2 = [Exchange("gx", us.at[c, 0:8], us.at[c, lead - 8:lead], yl2.at[c], yh2.at[c],
                   [y2_sem.at[c, k] for k in range(4)]) for c in range(nz)]
    g1 = Exchange("gy", q1.at[:, 8:16], q1.at[:, rows:rows + 8], q1.at[:, 0:8], q1.at[:, rows + 8:rows + 16],
                  [g1_sem.at[k] for k in range(4)])
    g2 = Exchange("gy", q2.at[:, 8:16], q2.at[:, rows:rows + 8], q2.at[:, 0:8], q2.at[:, rows + 8:rows + 16],
                  [g2_sem.at[k] for k in range(4)])
    states = (st0, st1, st2)
    xs, rs, cs = [], [], []
    for r in range(3):
        which = slice(1, 2) if r == 2 else slice(0, 2)
        xs.append(Exchange("gx", states[r].at[which, 0], states[r].at[which, lead - 1],
                           lx_lo.at[r, which], lx_hi.at[r, which], [x_sem.at[r, k] for k in range(4)]))
        rs.append(Exchange("gy", ys.at[r, 0], ys.at[r, 1], yl.at[r, 0], yl.at[r, 1], [r_sem.at[r, k] for k in range(4)]))
        cs.append(Exchange("gz", zsnd.at[r, 0], zsnd.at[r, 1], zl.at[r, 0], zl.at[r, 1], [c_sem.at[r, k] for k in range(4)]))
    for e in y1 + y2 + [g1, g2] + xs + rs + cs:
        e.clear()

    loads[0].wait()

    def smooth_z1(i, carry):
        x = jnp.concatenate([mat[i], jnp.zeros((thin, 128), F32)], axis=1)
        x = tri_lanes(x)
        for c in range(nz):
            zs[c, i] = x[:, c * cols:(c + 1) * cols]
        return carry

    lax.fori_loop(0, lead, smooth_z1, 0)

    pl.semaphore_wait(barrier, (nz - 1) + (gx > 0).astype(jnp.int32) + (gx < nx - 1).astype(jnp.int32)
                      + (gy > 0).astype(jnp.int32) + (gy < ny - 1).astype(jnp.int32))

    def chunk_copy(src, dst, c, slot, sems):
        return pltpu.make_async_remote_copy(src_ref=src, dst_ref=dst, send_sem=sems.at[0, slot], recv_sem=sems.at[1, slot],
                                            device_id={"gz": c}, device_id_type=MESH)

    def tile_rows(g):
        return pl.ds(pl.multiple_of(8 + thin * g, 8), thin)

    def y_exchange(src, low, high, c, sems):
        return Exchange("gx", src.at[c, 0:8], src.at[c, lead - 8:lead], low.at[c], high.at[c], [sems.at[c, k] for k in range(4)])

    def order(t):
        return lax.rem(gz + 1 + t, nz)

    for t in range(nz):
        y_exchange(zs, yl1, yh1, order(t), y1_sem).start()

    loads[1].wait()
    loads[2].wait()
    xs[0].start()
    row_at = lax.broadcasted_iota(jnp.int32, (rows, cols), 0)
    lane_at = lax.broadcasted_iota(jnp.int32, (rows, cols), 1)
    lane_128 = lax.broadcasted_iota(jnp.int32, (rows, 128), 1)

    def pack(r, i, k, field, sides):
        at = k * lead + i
        ys[r, 0, pl.ds(at, 1), :] = field[0:1, :]
        ys[r, 1, pl.ds(at, 1), :] = field[rows - 1:rows, :]
        low, high = sides
        low = jnp.where(lane_128 == at, pltpu.roll(field[:, 0:128], at, 1), low)
        high = jnp.where(lane_128 == at, pltpu.roll(field[:, cols - 128:cols], at + 1, 1), high)
        return low, high

    def pack_first(i, sides):
        sides = pack(0, i, 0, st0[0, i], sides)
        return pack(0, i, 1, st0[1, i], sides)

    blank = (jnp.zeros((rows, 128), F32), jnp.zeros((rows, 128), F32))
    sides = lax.fori_loop(0, lead, pack_first, blank)
    zsnd[0, 0], zsnd[0, 1] = sides
    rs[0].start()
    cs[0].start()

    def smooth_lead(src, low, high, c, dst):
        for a in range(thin // 8):
            for b in range(cols // 128):
                part = (slice(None), slice(8 * a, 8 * a + 8), slice(128 * b, 128 * b + 128))
                x = jnp.concatenate([low[(c,) + part], src[(c,) + part], high[(c,) + part]], axis=0)
                dst(part, tri_lead(x))

    for t in range(nz):
        c = order(t)
        y_exchange(zs, yl1, yh1, c, y1_sem).wait()
        if t < nz - 1:
            def put(part, value):
                ds[(c,) + part] = value
            smooth_lead(zs, yl1, yh1, c, put)
            chunk_copy(ds.at[c], q1.at[:, tile_rows(gz), :], c, t, a1_sem).start()
        else:
            def put(part, value):
                q1[:, pl.ds(pl.multiple_of(8 + thin * gz + part[1].start, 8), 8), part[2]] = value
            smooth_lead(zs, yl1, yh1, c, put)
    for t in range(nz - 1):
        source = lax.rem(gz - 1 - t + nz, nz)
        chunk_copy(ds.at[source], q1.at[:, tile_rows(source), :], source, t, a1_sem).wait_recv()

    g1.start()
    for k in (3, 4, 5):
        loads[k].wait()
    g1.wait()

    def project(i, carry):
        x = tri_rows(q1[i]) * SCALE
        th = jnp.tanh(4.0 * (x - 0.5))
        dens = (TANH2 + th) * (0.5 / TANH2)
        slop = (1.0 - th * th) * (2.0 / TANH2)
        inv = 1.0 / (0.5 + dens)
        rinv[i] = 1.0 / (6.0 + 2.0 * (1.0 - dens) * inv)
        cond[i] = 1.0 - 0.8 * dens
        gain[i] = -3.0 * inv * inv * slop
        slope[i] = slop
        return carry

    lax.fori_loop(0, lead, project, 0)

    def beside(r, k, i, field):
        at = k * lead + i
        up = jnp.where(row_at == 0, yl[r, 0, pl.ds(at, 1), :], pltpu.roll(field, 1, 0))
        down = jnp.where(row_at == rows - 1, yl[r, 1, pl.ds(at, 1), :], pltpu.roll(field, rows - 1, 0))
        low = pltpu.roll(zl[r, 0], lax.rem(128 - at, 128), 1)
        high = pltpu.roll(zl[r, 1], 127 - at, 1)
        left, right = pltpu.roll(field, 1, 1), pltpu.roll(field, cols - 1, 1)
        left = jnp.concatenate([jnp.where(lane_128 == 0, low, left[:, 0:128]), left[:, 128:]], axis=1)
        right = jnp.concatenate([right[:, :cols - 128], jnp.where(lane_128 == 127, high, right[:, cols - 128:])], axis=1)
        return up, down, left, right

    def sweep(r, i, before, after):
        old, new = states[r], states[r + 1]
        s, t = old[0, i], old[1, i]
        upwind = before(1)
        marks = mark[i]
        a, b, c, d = beside(r, 0, i, s)
        total = before(0) + after(0) + ((a + b) + (c + d))
        fresh_s = (press[i] + total) * rinv[i]
        fresh_s = jnp.where(marks == 1, 1.0, jnp.where(marks == 2, 0.0, fresh_s))
        a, b, c, d = beside(r, 1, i, t)
        total = upwind + after(1) + ((a + b) + (c + d))
        h, drift = cond[i], 2.0 * s
        fresh_t = (warm[i] + h * total + drift * upwind) / (6.0 * h + drift + 0.1)
        fresh_t = jnp.where(marks == 1, 0.0, fresh_t)
        new[0, i], new[1, i] = fresh_s, fresh_t
        return fresh_s, fresh_t

    def run_sweep(r):
        old = states[r]

        def packed(i, sides, fresh):
            if r == 0:
                sides = pack(1, i, 0, fresh[0], sides)
            return pack(r + 1, i, 1, fresh[1], sides)

        def inner(i, sides):
            return packed(i, sides, sweep(r, i, lambda k: old[k, i - 1], lambda k: old[k, i + 1]))

        rs[r].wait()
        cs[r].wait()
        if r == 0:
            xs[r].wait()
        else:
            sides = lax.fori_loop(1, lead - 1, inner, blank)
            xs[r].wait()
        first = sweep(r, 0, lambda k: lx_lo[r, k], lambda k: old[k, 1])
        last = sweep(r, lead - 1, lambda k: old[k, lead - 2], lambda k: lx_hi[r, k])
        xs[r + 1].start()
        if r == 0:
            sides = packed(0, blank, first)
            sides = packed(lead - 1, sides, last)
            sides = lax.fori_loop(1, lead - 1, inner, sides)
        else:
            sides = packed(0, sides, first)
            sides = packed(lead - 1, sides, last)
        zsnd[r + 1, 0], zsnd[r + 1, 1] = sides
        rs[r + 1].start()
        cs[r + 1].start()

    ys[2] = jnp.zeros(ys.shape[1:], F32)
    run_sweep(0)
    run_sweep(1)
    stores = [pltpu.make_async_copy(st2.at[0], speed_o, out_sem.at[0]), pltpu.make_async_copy(st2.at[1], temper_o, out_sem.at[1])]
    for store in stores:
        store.start()

    def spread(i, before, after):
        s, t = st2[0, i], st2[1, i]
        energy = (before - t) ** 2 + (after - t) ** 2
        for other in beside(2, 1, i, t):
            energy = energy + (other - t) ** 2
        q2[i, 8:rows + 8, :] = gain[i] * s * s - 0.4 * energy * slope[i]

    rs[2].wait()
    cs[2].wait()

    def inner_spread(i, carry):
        spread(i, st2[1, i - 1], st2[1, i + 1])
        return carry

    lax.fori_loop(1, lead - 1, inner_spread, 0)
    xs[2].wait()
    spread(0, lx_lo[2, 1], st2[1, 1])
    spread(lead - 1, st2[1, lead - 2], lx_hi[2, 1])
    g2.start()
    g2.wait()

    def smooth_rows(i, carry):
        x = tri_rows(q2[i])
        for c in range(nz):
            us[c, i] = x[c * thin:(c + 1) * thin, :]
        return carry

    lax.fori_loop(0, lead, smooth_rows, 0)
    for t in range(nz):
        y_exchange(us, yl2, yh2, order(t), y2_sem).start()
    for t in range(nz):
        c = order(t)
        y_exchange(us, yl2, yh2, c, y2_sem).wait()
        if t < nz - 1:
            def put(part, value):
                ws[(c,) + part] = value
            smooth_lead(us, yl2, yh2, c, put)
            chunk_copy(ws.at[c], slab.at[gz], c, t, a2_sem).start()
        else:
            def put(part, value):
                slab[(gz,) + part] = value
            smooth_lead(us, yl2, yh2, c, put)
    for t in range(nz - 1):
        source = lax.rem(gz - 1 - t + nz, nz)
        chunk_copy(ws.at[source], slab.at[source], source, t, a2_sem).wait_recv()

    def smooth_z2(i, carry):
        x = jnp.concatenate([slab[c, i] for c in range(nz)] + [jnp.zeros((thin, 128), F32)], axis=1)
        outs[i] = tri_lanes(x)[:, :nz * cols] * SCALE
        return carry

    lax.fori_loop(0, lead, smooth_z2, 0)
    stores.append(pltpu.make_async_copy(outs, deriv_o, out_sem.at[2]))
    stores[2].start()

    for e in y1 + y2 + [g1, g2] + xs + rs + cs:
        e.finish()
    for t in range(nz - 1):
        c = order(t)
        chunk_copy(ds.at[c], q1.at[:, tile_rows(gz), :], c, t, a1_sem).wait_send()
        chunk_copy(ws.at[c], slab.at[gz], c, t, a2_sem).wait_send()
    for store in stores:
        store.wait()


def solution(mesh):
    nz = mesh.shape["gz"]

    def body(mat, mark, press, warm, vel, temp):
        lead, rows, cols = vel.shape
        thin, full = mat.shape[1:]
        tile, flat = (lead, rows, cols), (lead, thin, full)
        dma = pltpu.SemaphoreType.DMA
        vmem = lambda *shape: pltpu.VMEM(shape, F32)
        chunks, half = (nz, lead, thin, cols), (nz, 8, thin, cols)
        return pl.pallas_call(
            kernel,
            name="design_iteration",
            out_shape=[jax.ShapeDtypeStruct(tile, F32), jax.ShapeDtypeStruct(tile, F32), jax.ShapeDtypeStruct(flat, F32)],
            in_specs=[pl.BlockSpec(memory_space=pl.ANY)] * 6,
            out_specs=[pl.BlockSpec(memory_space=pl.ANY)] * 3,
            scratch_shapes=[
                vmem(*flat), pltpu.VMEM(tile, jnp.int32), vmem(*tile), vmem(*tile),
                vmem(2, *tile), vmem(2, *tile), vmem(2, *tile),
                vmem(*tile), vmem(*tile), vmem(*tile), vmem(*tile),
                vmem(*chunks), vmem(*half), vmem(*half), vmem(*chunks),
                vmem(lead, rows + 16, cols), vmem(lead, rows + 16, cols),
                vmem(*chunks), vmem(*half), vmem(*half), vmem(*chunks), vmem(*chunks), vmem(*flat),
                vmem(3, 2, rows, cols), vmem(3, 2, rows, cols),
                vmem(3, 2, 2 * lead, cols), vmem(3, 2, 2 * lead, cols),
                vmem(3, 2, rows, 128), vmem(3, 2, rows, 128),
                dma((6,)), dma((3,)), dma((nz, 4)), dma((nz, 4)), dma((4,)), dma((4,)),
                dma((2, nz)), dma((2, nz)), dma((3, 4)), dma((3, 4)), dma((3, 4)),
            ],
            compiler_params=pltpu.CompilerParams(
                collective_id=0, has_side_effects=True, vmem_limit_bytes=48 * 1024 * 1024),
        )(mat, mark, press, warm, vel, temp)

    tiles, slabs = P("gx", "gy", "gz"), P("gx", ("gy", "gz"), None)
    return jax.shard_map(body, mesh=mesh, in_specs=(slabs,) + (tiles,) * 5, out_specs=(tiles, tiles, slabs), check_vma=False)
```

profile of v0, /device:TPU:27, one launch (start us, length us, event | category | flops | bytes accessed | tf_op | source)
XLA Modules:
  0.0 120.8 jit_solution(331818784998866018)
XLA Ops:
  0.6 0.0 copy-start
  0.6 1.2 %copy-done = f32[16,16,1024]{2,1,0:T(8,128)S(1)} copy-done((f32[16,16,1024]{2,1,0:T(8,128)S(1)}, f32[16,16,1024]{2,1,0:T(8,128)}, u32[]{:S(2)}) %copy-start) | copy-done | bytes 1048600
  1.9 0.0 copy-start.1
  1.9 1.2 %copy-done.1 = s32[16,64,256]{2,1,0:T(8,128)S(1)} copy-done((s32[16,64,256]{2,1,0:T(8,128)S(1)}, s32[16,64,256]{2,1,0:T(8,128)}, u32[]{:S(2)}) %copy-start.1) | copy-done | bytes 1048600
  3.1 114.8 %design_iteration.1 = (f32[16,64,256]{2,1,0:T(8,128)S(1)}, f32[16,64,256]{2,1,0:T(8,128)S(1)}, f32[16,16,1024]{2,1,0:T(8,128)S(1)}) custom-call(f32[16,16,1024]{2,1,0:T(8,128)S(1)} %copy-done, s32[16,64,256]{2,1,0:T(8,128)S(1)} %copy-done.1, f32[16,64,256]{2,1,0:T(8,128)} %press_h.1, f32[16,64,256]{2,1,0:T(8,128)} %warm_h.1, f32[16,64,256]{2,1,0:T(8,128)} %vel_h.1, ...), custom_call_target="tpu_custom_call" | custom-call | tf_op jit(solution)/shard_map/design_iteration/pallas_call | solution.py:399
  117.9 1.0 copy.12
  118.8 1.0 copy.13
  119.8 1.0 copy.14
Async XLA Ops:
  0.6 1.2 %copy-start = (f32[16,16,1024]{2,1,0:T(8,128)S(1)}, f32[16,16,1024]{2,1,0:T(8,128)}, u32[]{:S(2)}) copy-start(f32[16,16,1024]{2,1,0:T(8,128)} %mat_h.1) | copy-start | bytes 3145732
  1.9 1.2 %copy-start.1 = (s32[16,64,256]{2,1,0:T(8,128)S(1)}, s32[16,64,256]{2,1,0:T(8,128)}, u32[]{:S(2)}) copy-start(s32[16,64,256]{2,1,0:T(8,128)} %mark_h.1) | copy-start | bytes 3145732
where the time goes:
time: 121 us
  Pallas kernels  115 us (95%)
  local copies, waits for them, and re-layouts  5.35 us (4%)
    pallas_call x1, Pallas kernels, body(): pl.pallas_call(kernel, name='design_iteration', out_shape=[jax.ShapeDtype...  115 us
    unnamed x7, local copies, waits for them, and re-layouts  5.35 us

commit v1 on v0

v1 whole, which is shorter than its diff:
```python
import functools
import math

import jax
import jax.numpy as jnp
from jax import lax
from jax.experimental import pallas as pl
from jax.experimental.pallas import tpu as pltpu
from jax.sharding import PartitionSpec as P

MESH = pl.DeviceIdType.MESH
F32 = jnp.float32

TANH2 = math.tanh(2.0)
GROUP = 4
SCALE = 1.0 / 81.0**3


def band_rows(n):
    row = lax.broadcasted_iota(jnp.int32, (n + 256, n), 0)
    col = lax.broadcasted_iota(jnp.int32, (n + 256, n), 1)
    return jnp.maximum(9 - jnp.abs(row - 128 - col), 0).astype(F32).astype(jnp.bfloat16)


def tri_lanes(x, band):
    top = x.astype(jnp.bfloat16)
    rest = x - top.astype(F32)
    mid = rest.astype(jnp.bfloat16)
    low = (rest - mid.astype(F32)).astype(jnp.bfloat16)
    y = jnp.dot(jnp.concatenate([top, mid, low], axis=0), band, preferred_element_type=F32)
    n = x.shape[0]
    return y[:n] + (y[n:2 * n] + y[2 * n:])


def tri_rows(x):
    n = x.shape[0]
    a = x + pltpu.roll(x, 1, 0)
    a = a + pltpu.roll(a, 2, 0)
    a = a + pltpu.roll(a, 4, 0)
    a = a + pltpu.roll(x, 8, 0)
    b = a + pltpu.roll(a, 1, 0)
    b = b + pltpu.roll(b, 2, 0)
    b = b + pltpu.roll(b, 4, 0)
    b = b + pltpu.roll(a, 8, 0)
    return b[16:]


def box_lead(x):
    a = x[1:] + x[:-1]
    a = a[2:] + a[:-2]
    a = a[4:] + a[:-4]
    return a[1:] + x[: x.shape[0] - 8]


def tri_lead(x):
    return box_lead(box_lead(x))


def when(condition, act):
    if condition is None:
        act()
    else:
        pl.when(condition)(act)


class Copy:
    def __init__(self, src, dst, sems, target, sends=None, receives=None, here=None):
        self.src, self.dst, self.sems, self.target = src, dst, sems, target
        self.sends, self.receives, self.here = sends, receives, dst if here is None else here

    def make(self, dst):
        return pltpu.make_async_remote_copy(src_ref=self.src, dst_ref=dst, send_sem=self.sems[0], recv_sem=self.sems[1],
                                            device_id=self.target, device_id_type=MESH)

    def start(self):
        when(self.sends, lambda: self.make(self.dst).start())

    def wait(self):
        when(self.receives, lambda: self.make(self.here).wait_recv())

    def finish(self):
        when(self.sends, lambda: self.make(self.dst).wait_send())


def kernel(mat_h, mark_h, press_h, warm_h, vel_h, temp_h, speed_o, temper_o, deriv_o,
           mat, mark, press, warm, st0, st1, st2, rinv, cond, gain, slope, band,
           zs, yl1, yh1, ds, q1, q2, us, yl2, yh2, ws, slab, outs, fy1, fy2,
           lx_lo, lx_hi, ys, yl, zsnd, zl, in_sem, out_sem, link_sem):
    gx, gy, gz = lax.axis_index("gx"), lax.axis_index("gy"), lax.axis_index("gz")
    nx, ny, nz = lax.axis_size("gx"), lax.axis_size("gy"), lax.axis_size("gz")
    lead, rows, cols = st0.shape[1:]
    thin = rows // nz
    full = nz * cols

    loads = [pltpu.make_async_copy(src, dst, in_sem.at[k]) for k, (src, dst) in enumerate(
        [(mat_h, mat), (vel_h, st0.at[0]), (temp_h, st0.at[1]), (press_h, press), (warm_h, warm), (mark_h, mark)])]
    for load in loads:
        load.start()

    edge_first, edge_last = lax.rem(gx, GROUP) == 0, lax.rem(gx, GROUP) == GROUP - 1
    at_edge = jnp.logical_or(edge_first, edge_last)
    both = jnp.logical_and
    has_before, has_after = gx >= GROUP, gx < nx - GROUP
    partners = [("gx", gx - 1, gx > 0), ("gx", gx + 1, gx < nx - 1), ("gy", gy - 1, gy > 0), ("gy", gy + 1, gy < ny - 1)]
    if nx > GROUP:
        partners += [("gx", gx - GROUP, both(at_edge, has_before)), ("gx", gx + GROUP, both(at_edge, has_after)),
                     ("gx", gx + GROUP - 1, edge_first), ("gx", gx - GROUP + 1, edge_last)]
    barrier = pltpu.get_barrier_semaphore()
    greeted = jnp.int32(nz - 1)
    for axis, to, there in partners:
        def greet():
            pl.semaphore_signal(barrier, inc=1, device_id={axis: to}, device_id_type=MESH)
        pl.when(there)(greet)
        greeted = greeted + there.astype(jnp.int32)
    for hop in range(1, nz):
        pl.semaphore_signal(barrier, inc=1, device_id={"gz": lax.rem(gz + hop, nz)}, device_id_type=MESH)

    used = [0]

    def sems():
        used[0] += 1
        return link_sem.at[0, used[0] - 1], link_sem.at[1, used[0] - 1]

    started = []

    def start(*copies):
        for copy in copies:
            copy.start()
            started.append(copy)

    def wait(*copies):
        for copy in copies:
            copy.wait()

    def finish(*copies):
        for copy in copies:
            copy.finish()
            started.remove(copy)

    def begin_lead(halos, *steps):
        for t in steps:
            near, legs_in, _ = halos[t]
            start(*legs_in, *near)

    def exchange(axis, low, high, land_low, land_high):
        at, count = lax.axis_index(axis), lax.axis_size(axis)

        @pl.when(at == 0)
        def _():
            land_low[...] = jnp.zeros(land_low.shape, F32)

        @pl.when(at == count - 1)
        def _():
            land_high[...] = jnp.zeros(land_high.shape, F32)

        return (Copy(high, land_low, sems(), {axis: at + 1}, at < count - 1, at > 0),
                Copy(low, land_high, sems(), {axis: at - 1}, at > 0, at < count - 1))

    hops = [2, 1, 3, 0] if nz == 4 else list(range(1, nz)) + [0]
    order = [lax.rem(gz + hop, nz) for hop in hops]

    def lead_halos(src, low, high, held):
        @pl.when(gx == 0)
        def _():
            low[...] = jnp.zeros(low.shape, F32)

        @pl.when(gx == nx - 1)
        def _():
            high[...] = jnp.zeros(high.shape, F32)

        h = thin // 2
        plans = []
        for t in range(nz):
            c = order[t]
            near, legs_in, legs_out = [], [], []
            for up in (True, False):
                out = src.at[c, lead - 8:lead] if up else src.at[c, 0:8]
                land = (low if up else high).at[c]
                step = 1 if up else -1
                sends, receives = (gx < nx - 1, gx > 0) if up else (gx > 0, gx < nx - 1)
                crosses = both(edge_last, sends) if up else both(edge_first, sends)
                if nx > GROUP:
                    near.append(Copy(out.at[:, 0:h], land.at[:, 0:h], sems(), {"gx": gx + step}, sends, receives))
                    pair = sems()
                    direct = both(sends, jnp.logical_not(crosses))
                    near.append(Copy(out.at[:, h:], land.at[:, h:], pair, {"gx": gx + step}, direct, receives))
                    first, second = -step * (GROUP - 1), step * GROUP
                    holds = both(edge_first, has_after) if up else both(edge_last, has_before)
                    legs_in.append(Copy(out.at[:, h:], held.at[t], sems(), {"gx": gx + first}, crosses, holds))
                    legs_out.append(Copy(held.at[t], land.at[:, h:], (sems()[0], pair[1]), {"gx": gx + second}, holds))
                else:
                    near.append(Copy(out, land, sems(), {"gx": gx + step}, sends, receives))
            plans.append((near, legs_in, legs_out))
        return plans

    def to_chunks(src, place):
        return [Copy(src.at[order[t]], place(gz), sems(), {"gz": order[t]}, here=place(lax.rem(gz + nz - hops[t], nz)))
                for t in range(nz - 1)]

    def tile_rows(g):
        return q1.at[:, pl.ds(pl.multiple_of(8 + thin * g, 8), thin), :]

    y1, y2 = lead_halos(zs, yl1, yh1, fy1), lead_halos(us, yl2, yh2, fy2)
    a1, a2 = to_chunks(ds, tile_rows), to_chunks(ws, lambda g: slab.at[g])
    g1 = exchange("gy", q1.at[:, 8:16], q1.at[:, rows:rows + 8], q1.at[:, 0:8], q1.at[:, rows + 8:rows + 16])
    g2 = exchange("gy", q2.at[:, 8:16], q2.at[:, rows:rows + 8], q2.at[:, 0:8], q2.at[:, rows + 8:rows + 16])
    states = (st0, st1, st2)
    xs, rs, cs = [], [], []
    for r in range(3):
        which = slice(1, 2) if r == 2 else slice(0, 2)
        xs.append(exchange("gx", states[r].at[which, 0], states[r].at[which, lead - 1], lx_lo.at[r, which], lx_hi.at[r, which]))
        rs.append(exchange("gy", ys.at[r, 0], ys.at[r, 1], yl.at[r, 0], yl.at[r, 1]))
        cs.append(exchange("gz", zsnd.at[r, 0], zsnd.at[r, 1], zl.at[r, 0], zl.at[r, 1]))

    def smooth_full(piece, c, m):
        first, last = max(0, c * cols - 128), min(full, (c + 1) * cols + 128)
        skip = first - (c * cols - 128)
        x = piece(pl.ds(8 * m, 8), first, last).reshape(8 * thin, last - first)
        return tri_lanes(x, band[skip:skip + last - first, :]).reshape(8, thin, cols)

    band[...] = band_rows(cols)
    loads[0].wait()

    def smooth_z1(m, carry):
        for c in range(nz):
            zs[c, pl.ds(8 * m, 8)] = smooth_full(lambda at, a, b: mat[at, :, a:b], c, m)
        return carry

    lax.fori_loop(0, lead // 8, smooth_z1, 0)
    pl.semaphore_wait(barrier, greeted)
    begin_lead(y1, 0, 1)

    loads[1].wait()
    loads[2].wait()
    start(*xs[0])
    row_at = lax.broadcasted_iota(jnp.int32, (rows, cols), 0)
    lane_128 = lax.broadcasted_iota(jnp.int32, (rows, 128), 1)

    def pack(r, i, k, field, sides):
        at = k * lead + i
        ys[r, 0, pl.ds(at, 1), :] = field[0:1, :]
        ys[r, 1, pl.ds(at, 1), :] = field[rows - 1:rows, :]
        low, high = sides
        low = jnp.where(lane_128 == at, pltpu.roll(field[:, 0:128], at, 1), low)
        high = jnp.where(lane_128 == at, pltpu.roll(field[:, cols - 128:cols], at + 1, 1), high)
        return low, high

    def pack_first(i, sides):
        sides = pack(0, i, 0, st0[0, i], sides)
        return pack(0, i, 1, st0[1, i], sides)

    blank = (jnp.zeros((rows, 128), F32), jnp.zeros((rows, 128), F32))
    sides = lax.fori_loop(0, lead, pack_first, blank, unroll=2)
    zsnd[0, 0], zsnd[0, 1] = sides
    start(*rs[0], *cs[0])

    def smooth_lead(src, low, high, c, put):
        for a in range(thin // 8):
            for b in range(cols // 128):
                part = (slice(None), slice(8 * a, 8 * a + 8), slice(128 * b, 128 * b + 128))
                x = jnp.concatenate([low[(c,) + part], src[(c,) + part], high[(c,) + part]], axis=0)
                put(part, tri_lead(x))

    def lead_then_chunks(halos, chunks, src, low, high, dst, put_own):
        for t in range(nz):
            c = order[t]
            near, legs_in, legs_out = halos[t]
            for leg_in, leg_out in zip(legs_in, legs_out):
                wait(leg_in)
                start(leg_out)
            if t + 2 < nz:
                finish(*legs_in, *near)
                begin_lead(halos, t + 2)
            wait(*near)
            if t < nz - 1:
                def put(part, value):
                    dst[(c,) + part] = value
                smooth_lead(src, low, high, c, put)
                start(chunks[t])
            else:
                smooth_lead(src, low, high, c, put_own)
        wait(*chunks)

    def put_tile(part, value):
        q1[:, pl.ds(pl.multiple_of(8 + thin * gz + part[1].start, 8), 8), part[2]] = value

    lead_then_chunks(y1, a1, zs, yl1, yh1, ds, put_tile)

    start(*g1)
    for k in (3, 4, 5):
        loads[k].wait()
    wait(*g1)

    def project(i, carry):
        x = tri_rows(q1[i]) * SCALE
        th = jnp.tanh(4.0 * (x - 0.5))
        dens = (TANH2 + th) * (0.5 / TANH2)
        slop = (1.0 - th * th) * (2.0 / TANH2)
        inv = 1.0 / (0.5 + dens)
        rinv[i] = 1.0 / (6.0 + 2.0 * (1.0 - dens) * inv)
        cond[i] = 1.0 - 0.8 * dens
        gain[i] = -3.0 * inv * inv * slop
        slope[i] = slop
        return carry

    lax.fori_loop(0, lead, project, 0)

    def beside(r, k, i, field):
        at = k * lead + i
        up = jnp.where(row_at == 0, yl[r, 0, pl.ds(at, 1), :], pltpu.roll(field, 1, 0))
        down = jnp.where(row_at == rows - 1, yl[r, 1, pl.ds(at, 1), :], pltpu.roll(field, rows - 1, 0))
        low = pltpu.roll(zl[r, 0], lax.rem(128 - at, 128), 1)
        high = pltpu.roll(zl[r, 1], 127 - at, 1)
        left, right = pltpu.roll(field, 1, 1), pltpu.roll(field, cols - 1, 1)
        left = jnp.concatenate([jnp.where(lane_128 == 0, low, left[:, 0:128]), left[:, 128:]], axis=1)
        right = jnp.concatenate([right[:, :cols - 128], jnp.where(lane_128 == 127, high, right[:, cols - 128:])], axis=1)
        return up, down, left, right

    def sweep(r, i, before, after):
        old, new = states[r], states[r + 1]
        s, t = old[0, i], old[1, i]
        upwind = before(1)
        marks = mark[i]
        a, b, c, d = beside(r, 0, i, s)
        total = before(0) + after(0) + ((a + b) + (c + d))
        fresh_s = (press[i] + total) * rinv[i]
        fresh_s = jnp.where(marks == 1, 1.0, jnp.where(marks == 2, 0.0, fresh_s))
        a, b, c, d = beside(r, 1, i, t)
        total = upwind + after(1) + ((a + b) + (c + d))
        h, drift = cond[i], 2.0 * s
        fresh_t = (warm[i] + h * total + drift * upwind) / (6.0 * h + drift + 0.1)
        fresh_t = jnp.where(marks == 1, 0.0, fresh_t)
        new[0, i], new[1, i] = fresh_s, fresh_t
        return fresh_s, fresh_t

    def run_sweep(r):
        old = states[r]

        def packed(i, sides, fresh):
            if r == 0:
                sides = pack(1, i, 0, fresh[0], sides)
            return pack(r + 1, i, 1, fresh[1], sides)

        def inner(i, sides):
            return packed(i, sides, sweep(r, i, lambda k: old[k, i - 1], lambda k: old[k, i + 1]))

        wait(*rs[r], *cs[r])
        if r > 0:
            sides = lax.fori_loop(1, lead - 1, inner, blank, unroll=2)
        wait(*xs[r])
        first = sweep(r, 0, lambda k: lx_lo[r, k], lambda k: old[k, 1])
        last = sweep(r, lead - 1, lambda k: old[k, lead - 2], lambda k: lx_hi[r, k])
        start(*xs[r + 1])
        if r == 0:
            sides = packed(0, blank, first)
            sides = packed(lead - 1, sides, last)
            sides = lax.fori_loop(1, lead - 1, inner, sides, unroll=2)
        else:
            sides = packed(0, sides, first)
            sides = packed(lead - 1, sides, last)
        zsnd[r + 1, 0], zsnd[r + 1, 1] = sides
        start(*rs[r + 1], *cs[r + 1])

    ys[2] = jnp.zeros(ys.shape[1:], F32)
    run_sweep(0)
    run_sweep(1)
    stores = [pltpu.make_async_copy(st2.at[0], speed_o, out_sem.at[0]), pltpu.make_async_copy(st2.at[1], temper_o, out_sem.at[1])]
    for store in stores:
        store.start()

    def spread(i, before, after):
        s, t = st2[0, i], st2[1, i]
        energy = (before - t) ** 2 + (after - t) ** 2
        for other in beside(2, 1, i, t):
            energy = energy + (other - t) ** 2
        q2[i, 8:rows + 8, :] = gain[i] * s * s - 0.4 * energy * slope[i]

    wait(*rs[2], *cs[2])

    def inner_spread(i, carry):
        spread(i, st2[1, i - 1], st2[1, i + 1])
        return carry

    lax.fori_loop(1, lead - 1, inner_spread, 0, unroll=2)
    wait(*xs[2])
    spread(0, lx_lo[2, 1], st2[1, 1])
    spread(lead - 1, st2[1, lead - 2], lx_hi[2, 1])
    start(*g2)
    wait(*g2)

    def smooth_rows(i, carry):
        x = tri_rows(q2[i])
        for c in range(nz):
            us[c, i] = x[c * thin:(c + 1) * thin, :]
        return carry

    lax.fori_loop(0, lead, smooth_rows, 0)
    begin_lead(y2, 0, 1)

    def put_slab(part, value):
        slab[(gz,) + part] = value

    lead_then_chunks(y2, a2, us, yl2, yh2, ws, put_slab)

    def columns(at, first, last):
        parts = []
        for c in range(nz):
            a, b = max(first, c * cols), min(last, (c + 1) * cols)
            if a < b:
                parts.append(slab[c, at, :, a - c * cols:b - c * cols])
        return jnp.concatenate(parts, axis=2)

    def smooth_z2(m, carry):
        for c in range(nz):
            outs[pl.ds(8 * m, 8), :, c * cols:(c + 1) * cols] = smooth_full(columns, c, m) * SCALE
        return carry

    lax.fori_loop(0, lead // 8, smooth_z2, 0)
    stores.append(pltpu.make_async_copy(outs, deriv_o, out_sem.at[2]))
    stores[2].start()

    for copy in started:
        copy.finish()
    for store in stores:
        store.wait()


def solution(mesh):
    nz = mesh.shape["gz"]

    def body(mat, mark, press, warm, vel, temp):
        lead, rows, cols = vel.shape
        thin, full = mat.shape[1:]
        tile, flat = (lead, rows, cols), (lead, thin, full)
        dma = pltpu.SemaphoreType.DMA
        vmem = lambda *shape: pltpu.VMEM(shape, F32)
        chunks, half = (nz, lead, thin, cols), (nz, 8, thin, cols)
        return pl.pallas_call(
            kernel,
            name="design_iteration",
            out_shape=[jax.ShapeDtypeStruct(tile, F32), jax.ShapeDtypeStruct(tile, F32), jax.ShapeDtypeStruct(flat, F32)],
            in_specs=[pl.BlockSpec(memory_space=pl.ANY)] * 6,
            out_specs=[pl.BlockSpec(memory_space=pl.ANY)] * 3,
            scratch_shapes=[
                vmem(*flat), pltpu.VMEM(tile, jnp.int32), vmem(*tile), vmem(*tile),
                vmem(2, *tile), vmem(2, *tile), vmem(2, *tile),
                vmem(*tile), vmem(*tile), vmem(*tile), vmem(*tile), pltpu.VMEM((cols + 256, cols), jnp.bfloat16),
                vmem(*chunks), vmem(*half), vmem(*half), vmem(*chunks),
                vmem(lead, rows + 16, cols), vmem(lead, rows + 16, cols),
                vmem(*chunks), vmem(*half), vmem(*half), vmem(*chunks), vmem(*chunks), vmem(*flat),
                vmem(nz, 8, thin // 2, cols), vmem(nz, 8, thin // 2, cols),
                vmem(3, 2, rows, cols), vmem(3, 2, rows, cols),
                vmem(3, 2, 2 * lead, cols), vmem(3, 2, 2 * lead, cols),
                vmem(3, 2, rows, 128), vmem(3, 2, rows, 128),
                dma((6,)), dma((3,)), dma((2, 104)),
            ],
            compiler_params=pltpu.CompilerParams(
                collective_id=0, has_side_effects=True, vmem_limit_bytes=60 * 1024 * 1024),
        )(mat, mark, press, warm, vel, temp)

    tiles, slabs = P("gx", "gy", "gz"), P("gx", ("gy", "gz"), None)
    return jax.shard_map(body, mesh=mesh, in_specs=(slabs,) + (tiles,) * 5, out_specs=(tiles, tiles, slabs), check_vma=False)
```

time: 121 us -> 99.8 us (0.82)
  the two profiles are of different devices: /device:TPU:27 before, /device:TPU:25 now
where the time goes in v1:
time: 99.8 us; the launch traced here: 99.7 us
  Pallas kernels  94 us (94%)
  local copies, waits for them, and re-layouts  4.96 us (5%)
    pallas_call x1, Pallas kernels, body(): pl.pallas_call(kernel, name='design_iteration', out_shape=[jax.ShapeDtype...  94 us
    unnamed x7, local copies, waits for them, and re-layouts  4.96 us

profile of v1, /device:TPU:25, one launch (start us, length us, event | category | flops | bytes accessed | tf_op | source)
XLA Modules:
  0.0 99.7 jit_solution(12680625023986885028)
XLA Ops:
  0.6 94.0 %design_iteration.1 = (f32[16,64,256]{2,1,0:T(8,128)}, f32[16,64,256]{2,1,0:T(8,128)}, f32[16,16,1024]{2,1,0:T(8,128)}) custom-call(f32[16,16,1024]{2,1,0:T(8,128)} %mat_h.1, s32[16,64,256]{2,1,0:T(8,128)} %mark_h.1, f32[16,64,256]{2,1,0:T(8,128)} %press_h.1, f32[16,64,256]{2,1,0:T(8,128)} %warm_h.1, f32[16,64,256]{2,1,0:T(8,128)} %vel_h.1, ...), custom_call_target="tpu_custom_call" | custom-call | tf_op jit(solution)/shard_map/design_iteration/pallas_call | solution.py:438
  94.7 0.0 copy-start.1
  94.7 2.4 %copy.12 = f32[16,64,256]{2,1,0:T(8,128)} copy(f32[16,64,256]{2,1,0:T(8,128)} %get-tuple-element.6) | data formatting | bytes 2097152
  97.1 0.0 copy-done.1
  97.1 0.0 copy-start
  97.1 1.0 copy.13
  98.1 0.6 copy-done
  98.7 1.0 copy.14
Async XLA Ops:
  94.7 2.4 %copy-start.1 = (f32[16,64,256]{2,1,0:T(8,128)S(1)}, f32[16,64,256]{2,1,0:T(8,128)}, u32[]{:S(2)}) copy-start(f32[16,64,256]{2,1,0:T(8,128)} %get-tuple-element.7) | copy-start | bytes 3145732
  97.1 1.6 %copy-start = (f32[16,16,1024]{2,1,0:T(8,128)S(1)}, f32[16,16,1024]{2,1,0:T(8,128)}, u32[]{:S(2)}) copy-start(f32[16,16,1024]{2,1,0:T(8,128)} %get-tuple-element.8) | copy-start | bytes 3145732

commit v2 on v1

--- a/solution.py
+++ b/solution.py
@@ -13,6 +13,7 @@
 
 TANH2 = math.tanh(2.0)
 GROUP = 4
+THROUGH = 3
 SCALE = 1.0 / 81.0**3
 
 
@@ -56,6 +57,13 @@
     return box_lead(box_lead(x))
 
 
+def smooth_full(piece, c, m, thin, cols, full, band):
+    first, last = max(0, c * cols - 128), min(full, (c + 1) * cols + 128)
+    skip = first - (c * cols - 128)
+    x = piece(pl.ds(8 * m, 8), first, last).reshape(8 * thin, last - first)
+    return tri_lanes(x, band[skip:skip + last - first, :]).reshape(8, thin, cols)
+
+
 def when(condition, act):
     if condition is None:
         act()
@@ -82,9 +90,9 @@
         when(self.sends, lambda: self.make(self.dst).wait_send())
 
 
-def kernel(mat_h, mark_h, press_h, warm_h, vel_h, temp_h, speed_o, temper_o, deriv_o,
+def kernel(mat_h, mark_h, press_h, warm_h, vel_h, temp_h, speed_o, temper_o, slab_o,
            mat, mark, press, warm, st0, st1, st2, rinv, cond, gain, slope, band,
-           zs, yl1, yh1, ds, q1, q2, us, yl2, yh2, ws, slab, outs, fy1, fy2,
+           zs, yl1, yh1, ds, q1, q2, us, yl2, yh2, ws, slab, fy1, fy2,
            lx_lo, lx_hi, ys, yl, zsnd, zl, in_sem, out_sem, link_sem):
     gx, gy, gz = lax.axis_index("gx"), lax.axis_index("gy"), lax.axis_index("gz")
     nx, ny, nz = lax.axis_size("gx"), lax.axis_size("gy"), lax.axis_size("gz")
@@ -137,10 +145,18 @@
             copy.finish()
             started.remove(copy)
 
-    def begin_lead(halos, *steps):
-        for t in steps:
-            near, legs_in, _ = halos[t]
-            start(*legs_in, *near)
+    def begin_lead(halos):
+        for near, legs_in, _ in halos:
+            start(*legs_in)
+        start(*halos[0][0])
+        pass_on(halos, 0)
+        start(*halos[1][0])
+
+    def pass_on(halos, t):
+        _, legs_in, legs_out = halos[t]
+        for leg_in, leg_out in zip(legs_in, legs_out):
+            wait(leg_in)
+            start(leg_out)
 
     def exchange(axis, low, high, land_low, land_high):
         at, count = lax.axis_index(axis), lax.axis_size(axis)
@@ -179,7 +195,7 @@
                 step = 1 if up else -1
                 sends, receives = (gx < nx - 1, gx > 0) if up else (gx > 0, gx < nx - 1)
                 crosses = both(edge_last, sends) if up else both(edge_first, sends)
-                if nx > GROUP:
+                if nx > GROUP and t < THROUGH:
                     near.append(Copy(out.at[:, 0:h], land.at[:, 0:h], sems(), {"gx": gx + step}, sends, receives))
                     pair = sems()
                     direct = both(sends, jnp.logical_not(crosses))
@@ -203,7 +219,9 @@
     y1, y2 = lead_halos(zs, yl1, yh1, fy1), lead_halos(us, yl2, yh2, fy2)
     a1, a2 = to_chunks(ds, tile_rows), to_chunks(ws, lambda g: slab.at[g])
     g1 = exchange("gy", q1.at[:, 8:16], q1.at[:, rows:rows + 8], q1.at[:, 0:8], q1.at[:, rows + 8:rows + 16])
-    g2 = exchange("gy", q2.at[:, 8:16], q2.at[:, rows:rows + 8], q2.at[:, 0:8], q2.at[:, rows + 8:rows + 16])
+    g2 = []
+    for part in (slice(1, lead - 1), slice(0, 1), slice(lead - 1, lead)):
+        g2.append(exchange("gy", q2.at[part, 8:16], q2.at[part, rows:rows + 8], q2.at[part, 0:8], q2.at[part, rows + 8:rows + 16]))
     states = (st0, st1, st2)
     xs, rs, cs = [], [], []
     for r in range(3):
@@ -212,23 +230,17 @@
         rs.append(exchange("gy", ys.at[r, 0], ys.at[r, 1], yl.at[r, 0], yl.at[r, 1]))
         cs.append(exchange("gz", zsnd.at[r, 0], zsnd.at[r, 1], zl.at[r, 0], zl.at[r, 1]))
 
-    def smooth_full(piece, c, m):
-        first, last = max(0, c * cols - 128), min(full, (c + 1) * cols + 128)
-        skip = first - (c * cols - 128)
-        x = piece(pl.ds(8 * m, 8), first, last).reshape(8 * thin, last - first)
-        return tri_lanes(x, band[skip:skip + last - first, :]).reshape(8, thin, cols)
-
     band[...] = band_rows(cols)
     loads[0].wait()
 
     def smooth_z1(m, carry):
         for c in range(nz):
-            zs[c, pl.ds(8 * m, 8)] = smooth_full(lambda at, a, b: mat[at, :, a:b], c, m)
+            zs[c, pl.ds(8 * m, 8)] = smooth_full(lambda at, a, b: mat[at, :, a:b], c, m, thin, cols, full, band)
         return carry
 
     lax.fori_loop(0, lead // 8, smooth_z1, 0)
     pl.semaphore_wait(barrier, greeted)
-    begin_lead(y1, 0, 1)
+    begin_lead(y1)
 
     loads[1].wait()
     loads[2].wait()
@@ -263,14 +275,12 @@
 
     def lead_then_chunks(halos, chunks, src, low, high, dst, put_own):
         for t in range(nz):
-            c = order[t]
-            near, legs_in, legs_out = halos[t]
-            for leg_in, leg_out in zip(legs_in, legs_out):
-                wait(leg_in)
-                start(leg_out)
+            c, near = order[t], halos[t][0]
+            if t + 1 < nz:
+                pass_on(halos, t + 1)
             if t + 2 < nz:
-                finish(*legs_in, *near)
-                begin_lead(halos, t + 2)
+                finish(*near)
+                start(*halos[t + 2][0])
             wait(*near)
             if t < nz - 1:
                 def put(part, value):
@@ -382,11 +392,12 @@
         return carry
 
     lax.fori_loop(1, lead - 1, inner_spread, 0, unroll=2)
+    start(*g2[0])
     wait(*xs[2])
     spread(0, lx_lo[2, 1], st2[1, 1])
     spread(lead - 1, st2[1, lead - 2], lx_hi[2, 1])
-    start(*g2)
-    wait(*g2)
+    start(*g2[1], *g2[2])
+    wait(*g2[0])
 
     def smooth_rows(i, carry):
         x = tri_rows(q2[i])
@@ -394,13 +405,34 @@
             us[c, i] = x[c * thin:(c + 1) * thin, :]
         return carry
 
-    lax.fori_loop(0, lead, smooth_rows, 0)
-    begin_lead(y2, 0, 1)
+    lax.fori_loop(1, lead - 1, smooth_rows, 0, unroll=2)
+    wait(*g2[1], *g2[2])
+    smooth_rows(0, 0)
+    smooth_rows(lead - 1, 0)
+    begin_lead(y2)
 
     def put_slab(part, value):
         slab[(gz,) + part] = value
 
     lead_then_chunks(y2, a2, us, yl2, yh2, ws, put_slab)
+
+    stores.append(pltpu.make_async_copy(slab, slab_o, out_sem.at[2]))
+    stores[2].start()
+
+    for copy in started:
+        copy.finish()
+    for store in stores:
+        store.wait()
+
+
+def last_kernel(speed_h, temper_h, slab_h, speed_o, temper_o, deriv_o, slab, outs, band, in_sem, out_sem):
+    nz, lead, thin, cols = slab.shape
+    moves = [pltpu.make_async_copy(speed_h, speed_o, out_sem.at[0]), pltpu.make_async_copy(temper_h, temper_o, out_sem.at[1])]
+    halves = [pl.ds(8 * m, 8) for m in range(lead // 8)]
+    loads = [pltpu.make_async_copy(slab_h.at[:, at], slab.at[:, at], in_sem.at[m]) for m, at in enumerate(halves)]
+    for copy in loads + moves:
+        copy.start()
+    band[...] = band_rows(cols)
 
     def columns(at, first, last):
         parts = []
@@ -410,19 +442,14 @@
                 parts.append(slab[c, at, :, a - c * cols:b - c * cols])
         return jnp.concatenate(parts, axis=2)
 
-    def smooth_z2(m, carry):
+    for m, at in enumerate(halves):
+        loads[m].wait()
         for c in range(nz):
-            outs[pl.ds(8 * m, 8), :, c * cols:(c + 1) * cols] = smooth_full(columns, c, m) * SCALE
-        return carry
-
-    lax.fori_loop(0, lead // 8, smooth_z2, 0)
-    stores.append(pltpu.make_async_copy(outs, deriv_o, out_sem.at[2]))
-    stores[2].start()
-
-    for copy in started:
-        copy.finish()
-    for store in stores:
-        store.wait()
+            outs[at, :, c * cols:(c + 1) * cols] = smooth_full(columns, c, m, thin, cols, nz * cols, band) * SCALE
+        moves.append(pltpu.make_async_copy(outs.at[at], deriv_o.at[at], out_sem.at[2 + m]))
+        moves[-1].start()
+    for move in moves:
+        move.wait()
 
 
 def solution(mesh):
@@ -435,10 +462,10 @@
         dma = pltpu.SemaphoreType.DMA
         vmem = lambda *shape: pltpu.VMEM(shape, F32)
         chunks, half = (nz, lead, thin, cols), (nz, 8, thin, cols)
-        return pl.pallas_call(
+        speed, temper, slab = pl.pallas_call(
             kernel,
             name="design_iteration",
-            out_shape=[jax.ShapeDtypeStruct(tile, F32), jax.ShapeDtypeStruct(tile, F32), jax.ShapeDtypeStruct(flat, F32)],
+            out_shape=[jax.ShapeDtypeStruct(tile, F32), jax.ShapeDtypeStruct(tile, F32), jax.ShapeDtypeStruct(chunks, F32)],
             in_specs=[pl.BlockSpec(memory_space=pl.ANY)] * 6,
             out_specs=[pl.BlockSpec(memory_space=pl.ANY)] * 3,
             scratch_shapes=[
@@ -447,16 +474,26 @@
                 vmem(*tile), vmem(*tile), vmem(*tile), vmem(*tile), pltpu.VMEM((cols + 256, cols), jnp.bfloat16),
                 vmem(*chunks), vmem(*half), vmem(*half), vmem(*chunks),
                 vmem(lead, rows + 16, cols), vmem(lead, rows + 16, cols),
-                vmem(*chunks), vmem(*half), vmem(*half), vmem(*chunks), vmem(*chunks), vmem(*flat),
+                vmem(*chunks), vmem(*half), vmem(*half), vmem(*chunks), vmem(*chunks),
                 vmem(nz, 8, thin // 2, cols), vmem(nz, 8, thin // 2, cols),
                 vmem(3, 2, rows, cols), vmem(3, 2, rows, cols),
                 vmem(3, 2, 2 * lead, cols), vmem(3, 2, 2 * lead, cols),
                 vmem(3, 2, rows, 128), vmem(3, 2, rows, 128),
-                dma((6,)), dma((3,)), dma((2, 104)),
+                dma((6,)), dma((3,)), dma((2, 112)),
             ],
             compiler_params=pltpu.CompilerParams(
                 collective_id=0, has_side_effects=True, vmem_limit_bytes=60 * 1024 * 1024),
         )(mat, mark, press, warm, vel, temp)
+        return pl.pallas_call(
+            last_kernel,
+            name="last_filter",
+            out_shape=[jax.ShapeDtypeStruct(tile, F32), jax.ShapeDtypeStruct(tile, F32), jax.ShapeDtypeStruct(flat, F32)],
+            in_specs=[pl.BlockSpec(memory_space=pl.ANY)] * 3,
+            out_specs=[pl.BlockSpec(memory_space=pl.ANY)] * 3,
+            scratch_shapes=[vmem(*chunks), vmem(*flat), pltpu.VMEM((cols + 256, cols), jnp.bfloat16),
+                            dma((lead // 8,)), dma((2 + lead // 8,))],
+            compiler_params=pltpu.CompilerParams(vmem_limit_bytes=48 * 1024 * 1024),
+        )(speed, temper, slab)
 
     tiles, slabs = P("gx", "gy", "gz"), P("gx", ("gy", "gz"), None)
     return jax.shard_map(body, mesh=mesh, in_specs=(slabs,) + (tiles,) * 5, out_specs=(tiles, tiles, slabs), check_vma=False)

time: 99.8 us -> 93.5 us (0.937)
  the two profiles are of different devices: /device:TPU:25 before, /device:TPU:121 now
where the time goes in v2:
time: 93.5 us; the launch traced here: 93.3 us
  Pallas kernels  89 us (95%)
  local copies, waits for them, and re-layouts  3.67 us (4%)
    pallas_call x1, Pallas kernels, body(): pl.pallas_call(kernel, name='design_iteration', out_shape=[jax.ShapeDtype...  86.8 us
    unnamed x6, local copies, waits for them, and re-layouts  3.67 us
    pallas_call x1, Pallas kernels, body(): pl.pallas_call(last_kernel, name='last_filter', out_shape=[jax.ShapeDtype...  2.24 us

profile of v2, /device:TPU:121, one launch (start us, length us, event | category | flops | bytes accessed | tf_op | source)
XLA Modules:
  0.0 93.3 jit_solution(7480682604280990299)
XLA Ops:
  0.6 86.8 %design_iteration.1 = (f32[16,64,256]{2,1,0:T(8,128)}, f32[16,64,256]{2,1,0:T(8,128)}, f32[4,16,16,256]{3,2,1,0:T(8,128)}) custom-call(f32[16,16,1024]{2,1,0:T(8,128)} %mat_h.1, s32[16,64,256]{2,1,0:T(8,128)} %mark_h.1, f32[16,64,256]{2,1,0:T(8,128)} %press_h.1, f32[16,64,256]{2,1,0:T(8,128)} %warm_h.1, f32[16,64,256]{2,1,0:T(8,128)} %vel_h.1, ...), custom_call_target="tpu_custom_call" | custom-call | tf_op jit(solution)/shard_map/design_iteration/pallas_call | solution.py:465
  87.4 0.0 copy-start
  87.4 1.2 %copy-done = f32[16,64,256]{2,1,0:T(8,128)S(1)} copy-done((f32[16,64,256]{2,1,0:T(8,128)S(1)}, f32[16,64,256]{2,1,0:T(8,128)}, u32[]{:S(2)}) %copy-start) | copy-done | bytes 1048600
  88.7 0.0 copy-start.1
  88.7 1.2 %copy-done.1 = f32[16,64,256]{2,1,0:T(8,128)S(1)} copy-done((f32[16,64,256]{2,1,0:T(8,128)S(1)}, f32[16,64,256]{2,1,0:T(8,128)}, u32[]{:S(2)}) %copy-start.1) | copy-done | bytes 1048600
  89.9 0.0 copy-start.2
  89.9 1.2 %copy-done.2 = f32[4,16,16,256]{3,2,1,0:T(8,128)S(1)} copy-done((f32[4,16,16,256]{3,2,1,0:T(8,128)S(1)}, f32[4,16,16,256]{3,2,1,0:T(8,128)}, u32[]{:S(2)}) %copy-start.2) | copy-done | bytes 1048600
  91.1 2.2 %last_filter.1 = (f32[16,64,256]{2,1,0:T(8,128)}, f32[16,64,256]{2,1,0:T(8,128)}, f32[16,16,1024]{2,1,0:T(8,128)}) custom-call(f32[16,64,256]{2,1,0:T(8,128)S(1)} %copy-done, f32[16,64,256]{2,1,0:T(8,128)S(1)} %copy-done.1, f32[4,16,16,256]{3,2,1,0:T(8,128)S(1)} %copy-done.2), custom_call_target="tpu_custom_call" | custom-call | tf_op jit(solution)/shard_map/last_filter/pallas_call | solution.py:487
Async XLA Ops:
  87.4 1.2 %copy-start = (f32[16,64,256]{2,1,0:T(8,128)S(1)}, f32[16,64,256]{2,1,0:T(8,128)}, u32[]{:S(2)}) copy-start(f32[16,64,256]{2,1,0:T(8,128)} %get-tuple-element.6.speed_h) | copy-start | bytes 3145732
  88.7 1.2 %copy-start.1 = (f32[16,64,256]{2,1,0:T(8,128)S(1)}, f32[16,64,256]{2,1,0:T(8,128)}, u32[]{:S(2)}) copy-start(f32[16,64,256]{2,1,0:T(8,128)} %get-tuple-element.7.temper_h) | copy-start | bytes 3145732
  89.9 1.2 %copy-start.2 = (f32[4,16,16,256]{3,2,1,0:T(8,128)S(1)}, f32[4,16,16,256]{3,2,1,0:T(8,128)}, u32[]{:S(2)}) copy-start(f32[4,16,16,256]{3,2,1,0:T(8,128)} %get-tuple-element.8.slab_h) | copy-start | bytes 3145732

commit v3 on v2

--- a/solution.py
+++ b/solution.py
@@ -244,7 +244,6 @@
 
     loads[1].wait()
     loads[2].wait()
-    start(*xs[0])
     row_at = lax.broadcasted_iota(jnp.int32, (rows, cols), 0)
     lane_128 = lax.broadcasted_iota(jnp.int32, (rows, 128), 1)
 
@@ -273,7 +272,7 @@
                 x = jnp.concatenate([low[(c,) + part], src[(c,) + part], high[(c,) + part]], axis=0)
                 put(part, tri_lead(x))
 
-    def lead_then_chunks(halos, chunks, src, low, high, dst, put_own):
+    def lead_then_chunks(halos, chunks, src, low, high, dst, put_own, late=()):
         for t in range(nz):
             c, near = order[t], halos[t][0]
             if t + 1 < nz:
@@ -281,6 +280,8 @@
             if t + 2 < nz:
                 finish(*near)
                 start(*halos[t + 2][0])
+            if t == max(nz - 3, 0):
+                start(*late)
             wait(*near)
             if t < nz - 1:
                 def put(part, value):
@@ -294,7 +295,7 @@
     def put_tile(part, value):
         q1[:, pl.ds(pl.multiple_of(8 + thin * gz + part[1].start, 8), 8), part[2]] = value
 
-    lead_then_chunks(y1, a1, zs, yl1, yh1, ds, put_tile)
+    lead_then_chunks(y1, a1, zs, yl1, yh1, ds, put_tile, xs[0])
 
     start(*g1)
     for k in (3, 4, 5):
@@ -425,14 +426,16 @@
         store.wait()
 
 
-def last_kernel(speed_h, temper_h, slab_h, speed_o, temper_o, deriv_o, slab, outs, band, in_sem, out_sem):
+def last_kernel(speed_h, temper_h, slab_h, speed_o, temper_o, deriv_o, speed, temper, slab, outs, band, in_sem, out_sem):
     nz, lead, thin, cols = slab.shape
-    moves = [pltpu.make_async_copy(speed_h, speed_o, out_sem.at[0]), pltpu.make_async_copy(temper_h, temper_o, out_sem.at[1])]
     halves = [pl.ds(8 * m, 8) for m in range(lead // 8)]
     loads = [pltpu.make_async_copy(slab_h.at[:, at], slab.at[:, at], in_sem.at[m]) for m, at in enumerate(halves)]
-    for copy in loads + moves:
-        copy.start()
+    for k, (src, dst) in enumerate([(speed_h, speed), (temper_h, temper)]):
+        loads.append(pltpu.make_async_copy(src, dst, in_sem.at[lead // 8 + k]))
+    for load in loads:
+        load.start()
     band[...] = band_rows(cols)
+    moves = []
 
     def columns(at, first, last):
         parts = []
@@ -448,6 +451,11 @@
             outs[at, :, c * cols:(c + 1) * cols] = smooth_full(columns, c, m, thin, cols, nz * cols, band) * SCALE
         moves.append(pltpu.make_async_copy(outs.at[at], deriv_o.at[at], out_sem.at[2 + m]))
         moves[-1].start()
+        if m == 0:
+            for k, (src, dst) in enumerate([(speed, speed_o), (temper, temper_o)]):
+                loads[lead // 8 + k].wait()
+                moves.append(pltpu.make_async_copy(src, dst, out_sem.at[k]))
+                moves[-1].start()
     for move in moves:
         move.wait()
 
@@ -490,9 +498,9 @@
             out_shape=[jax.ShapeDtypeStruct(tile, F32), jax.ShapeDtypeStruct(tile, F32), jax.ShapeDtypeStruct(flat, F32)],
             in_specs=[pl.BlockSpec(memory_space=pl.ANY)] * 3,
             out_specs=[pl.BlockSpec(memory_space=pl.ANY)] * 3,
-            scratch_shapes=[vmem(*chunks), vmem(*flat), pltpu.VMEM((cols + 256, cols), jnp.bfloat16),
-                            dma((lead // 8,)), dma((2 + lead // 8,))],
-            compiler_params=pltpu.CompilerParams(vmem_limit_bytes=48 * 1024 * 1024),
+            scratch_shapes=[vmem(*tile), vmem(*tile), vmem(*chunks), vmem(*flat), pltpu.VMEM((cols + 256, cols), jnp.bfloat16),
+                            dma((2 + lead // 8,)), dma((2 + lead // 8,))],
+            compiler_params=pltpu.CompilerParams(vmem_limit_bytes=62 * 1024 * 1024),
         )(speed, temper, slab)
 
     tiles, slabs = P("gx", "gy", "gz"), P("gx", ("gy", "gz"), None)

time: 93.5 us -> 86.7 us (0.927)
  the two profiles are of different devices: /device:TPU:121 before, /device:TPU:129 now
where the time goes in v3:
time: 86.7 us; the launch traced here: 86.6 us
  Pallas kernels  85.9 us (99%)
    pallas_call x1, Pallas kernels, body(): pl.pallas_call(kernel, name='design_iteration', out_shape=[jax.ShapeDtype...  82.6 us
    pallas_call x1, Pallas kernels, body(): pl.pallas_call(last_kernel, name='last_filter', out_shape=[jax.ShapeDtype...  3.32 us

profile of v3, /device:TPU:129, one launch (start us, length us, event | category | flops | bytes accessed | tf_op | source)
XLA Modules:
  0.0 86.6 jit_solution(14120586086240339097)
XLA Ops:
  0.6 82.6 %design_iteration.1 = (f32[16,64,256]{2,1,0:T(8,128)}, f32[16,64,256]{2,1,0:T(8,128)}, f32[4,16,16,256]{3,2,1,0:T(8,128)}) custom-call(f32[16,16,1024]{2,1,0:T(8,128)} %mat_h.1, s32[16,64,256]{2,1,0:T(8,128)} %mark_h.1, f32[16,64,256]{2,1,0:T(8,128)} %press_h.1, f32[16,64,256]{2,1,0:T(8,128)} %warm_h.1, f32[16,64,256]{2,1,0:T(8,128)} %vel_h.1, ...), custom_call_target="tpu_custom_call" | custom-call | tf_op jit(solution)/shard_map/design_iteration/pallas_call | solution.py:473
  83.3 3.3 %last_filter.1 = (f32[16,64,256]{2,1,0:T(8,128)}, f32[16,64,256]{2,1,0:T(8,128)}, f32[16,16,1024]{2,1,0:T(8,128)}) custom-call(f32[16,64,256]{2,1,0:T(8,128)} %get-tuple-element.6.speed_h, f32[16,64,256]{2,1,0:T(8,128)} %get-tuple-element.7.temper_h, f32[4,16,16,256]{3,2,1,0:T(8,128)} %get-tuple-element.8.slab_h), custom_call_target="tpu_custom_call" | custom-call | tf_op jit(solution)/shard_map/last_filter/pallas_call | solution.py:495

commit v4 on v3

--- a/solution.py
+++ b/solution.py
@@ -272,7 +272,7 @@
                 x = jnp.concatenate([low[(c,) + part], src[(c,) + part], high[(c,) + part]], axis=0)
                 put(part, tri_lead(x))
 
-    def lead_then_chunks(halos, chunks, src, low, high, dst, put_own, late=()):
+    def lead_then_chunks(halos, chunks, src, low, high, dst, put_own, late=(), landed=None):
         for t in range(nz):
             c, near = order[t], halos[t][0]
             if t + 1 < nz:
@@ -290,7 +290,12 @@
                 start(chunks[t])
             else:
                 smooth_lead(src, low, high, c, put_own)
-        wait(*chunks)
+                if landed is not None:
+                    landed(c)
+        for t in range(nz - 1):
+            wait(chunks[t])
+            if landed is not None:
+                landed(lax.rem(gz + nz - hops[t], nz))
 
     def put_tile(part, value):
         q1[:, pl.ds(pl.multiple_of(8 + thin * gz + part[1].start, 8), 8), part[2]] = value
@@ -415,10 +420,12 @@
     def put_slab(part, value):
         slab[(gz,) + part] = value
 
-    lead_then_chunks(y2, a2, us, yl2, yh2, ws, put_slab)
-
-    stores.append(pltpu.make_async_copy(slab, slab_o, out_sem.at[2]))
-    stores[2].start()
+    def store_slab(c):
+        stores.append(pltpu.make_async_copy(slab.at[c], slab_o.at[c], out_sem.at[len(stores)]))
+        stores[-1].start()
+
+    lead_then_chunks(y2, a2, us, yl2, yh2, ws, put_slab, landed=store_slab)
+
 
     for copy in started:
         copy.finish()
@@ -487,7 +494,7 @@
                 vmem(3, 2, rows, cols), vmem(3, 2, rows, cols),
                 vmem(3, 2, 2 * lead, cols), vmem(3, 2, 2 * lead, cols),
                 vmem(3, 2, rows, 128), vmem(3, 2, rows, 128),
-                dma((6,)), dma((3,)), dma((2, 112)),
+                dma((6,)), dma((2 + nz,)), dma((2, 112)),
             ],
             compiler_params=pltpu.CompilerParams(
                 collective_id=0, has_side_effects=True, vmem_limit_bytes=60 * 1024 * 1024),

time: 86.7 us -> 86.5 us (level)
  no operation moved by 1% of the time
where the time goes in v4:
time: 86.5 us
  Pallas kernels  85.8 us (99%)
    pallas_call x1, Pallas kernels, body(): pl.pallas_call(kernel, name='design_iteration', out_shape=[jax.ShapeDtype...  82.5 us
    pallas_call x1, Pallas kernels, body(): pl.pallas_call(last_kernel, name='last_filter', out_shape=[jax.ShapeDtype...  3.32 us

profile of v4, /device:TPU:129, one launch (start us, length us, event | category | flops | bytes accessed | tf_op | source)
XLA Modules:
  0.0 86.5 jit_solution(2234261063208260756)
XLA Ops:
  0.6 82.5 %design_iteration.1 = (f32[16,64,256]{2,1,0:T(8,128)}, f32[16,64,256]{2,1,0:T(8,128)}, f32[4,16,16,256]{3,2,1,0:T(8,128)}) custom-call(f32[16,16,1024]{2,1,0:T(8,128)} %mat_h.1, s32[16,64,256]{2,1,0:T(8,128)} %mark_h.1, f32[16,64,256]{2,1,0:T(8,128)} %press_h.1, f32[16,64,256]{2,1,0:T(8,128)} %warm_h.1, f32[16,64,256]{2,1,0:T(8,128)} %vel_h.1, ...), custom_call_target="tpu_custom_call" | custom-call | tf_op jit(solution)/shard_map/design_iteration/pallas_call | solution.py:480
  83.1 3.3 %last_filter.1 = (f32[16,64,256]{2,1,0:T(8,128)}, f32[16,64,256]{2,1,0:T(8,128)}, f32[16,16,1024]{2,1,0:T(8,128)}) custom-call(f32[16,64,256]{2,1,0:T(8,128)} %get-tuple-element.6.speed_h, f32[16,64,256]{2,1,0:T(8,128)} %get-tuple-element.7.temper_h, f32[4,16,16,256]{3,2,1,0:T(8,128)} %get-tuple-element.8.slab_h), custom_call_target="tpu_custom_call" | custom-call | tf_op jit(solution)/shard_map/last_filter/pallas_call | solution.py:502

commit v5 on v4

--- a/solution.py
+++ b/solution.py
@@ -172,7 +172,8 @@
         return (Copy(high, land_low, sems(), {axis: at + 1}, at < count - 1, at > 0),
                 Copy(low, land_high, sems(), {axis: at - 1}, at > 0, at < count - 1))
 
-    hops = [2, 1, 3, 0] if nz == 4 else list(range(1, nz)) + [0]
+    odd = lax.rem(gy, 2)
+    hops = [2, 1 + 2 * odd, 3 - 2 * odd, 0] if nz == 4 else list(range(1, nz)) + [0]
     order = [lax.rem(gz + hop, nz) for hop in hops]
 
     def lead_halos(src, low, high, held):

time: 86.5 us -> 87.2 us (level)
  no operation moved by 1% of the time
where the time goes in v5:
time: 87.2 us; the launch traced here: 86.3 us
  Pallas kernels  85.6 us (98%)
    pallas_call x1, Pallas kernels, body(): pl.pallas_call(kernel, name='design_iteration', out_shape=[jax.ShapeDtype...  82.3 us
    pallas_call x1, Pallas kernels, body(): pl.pallas_call(last_kernel, name='last_filter', out_shape=[jax.ShapeDtype...  3.32 us

profile of v5, /device:TPU:129, one launch (start us, length us, event | category | flops | bytes accessed | tf_op | source)
XLA Modules:
  0.0 86.3 jit_solution(10067391153186052179)
XLA Ops:
  0.6 82.3 %design_iteration.1 = (f32[16,64,256]{2,1,0:T(8,128)}, f32[16,64,256]{2,1,0:T(8,128)}, f32[4,16,16,256]{3,2,1,0:T(8,128)}) custom-call(f32[16,16,1024]{2,1,0:T(8,128)} %mat_h.1, s32[16,64,256]{2,1,0:T(8,128)} %mark_h.1, f32[16,64,256]{2,1,0:T(8,128)} %press_h.1, f32[16,64,256]{2,1,0:T(8,128)} %warm_h.1, f32[16,64,256]{2,1,0:T(8,128)} %vel_h.1, ...), custom_call_target="tpu_custom_call" | custom-call | tf_op jit(solution)/shard_map/design_iteration/pallas_call | solution.py:481
  83.0 3.3 %last_filter.1 = (f32[16,64,256]{2,1,0:T(8,128)}, f32[16,64,256]{2,1,0:T(8,128)}, f32[16,16,1024]{2,1,0:T(8,128)}) custom-call(f32[16,64,256]{2,1,0:T(8,128)} %get-tuple-element.6.speed_h, f32[16,64,256]{2,1,0:T(8,128)} %get-tuple-element.7.temper_h, f32[4,16,16,256]{3,2,1,0:T(8,128)} %get-tuple-element.8.slab_h), custom_call_target="tpu_custom_call" | custom-call | tf_op jit(solution)/shard_map/last_filter/pallas_call | solution.py:503

commit v6 on v4

--- a/solution.py
+++ b/solution.py
@@ -261,7 +261,7 @@
         return pack(0, i, 1, st0[1, i], sides)
 
     blank = (jnp.zeros((rows, 128), F32), jnp.zeros((rows, 128), F32))
-    sides = lax.fori_loop(0, lead, pack_first, blank, unroll=2)
+    sides = lax.fori_loop(0, lead, pack_first, blank, unroll=4)
     zsnd[0, 0], zsnd[0, 1] = sides
     start(*rs[0], *cs[0])
 
@@ -362,7 +362,7 @@
 
         wait(*rs[r], *cs[r])
         if r > 0:
-            sides = lax.fori_loop(1, lead - 1, inner, blank, unroll=2)
+            sides = lax.fori_loop(1, lead - 1, inner, blank, unroll=4)
         wait(*xs[r])
         first = sweep(r, 0, lambda k: lx_lo[r, k], lambda k: old[k, 1])
         last = sweep(r, lead - 1, lambda k: old[k, lead - 2], lambda k: lx_hi[r, k])
@@ -370,7 +370,7 @@
         if r == 0:
             sides = packed(0, blank, first)
             sides = packed(lead - 1, sides, last)
-            sides = lax.fori_loop(1, lead - 1, inner, sides, unroll=2)
+            sides = lax.fori_loop(1, lead - 1, inner, sides, unroll=4)
         else:
             sides = packed(0, sides, first)
             sides = packed(lead - 1, sides, last)
@@ -397,7 +397,7 @@
         spread(i, st2[1, i - 1], st2[1, i + 1])
         return carry
 
-    lax.fori_loop(1, lead - 1, inner_spread, 0, unroll=2)
+    lax.fori_loop(1, lead - 1, inner_spread, 0, unroll=4)
     start(*g2[0])
     wait(*xs[2])
     spread(0, lx_lo[2, 1], st2[1, 1])
@@ -411,7 +411,7 @@
             us[c, i] = x[c * thin:(c + 1) * thin, :]
         return carry
 
-    lax.fori_loop(1, lead - 1, smooth_rows, 0, unroll=2)
+    lax.fori_loop(1, lead - 1, smooth_rows, 0, unroll=4)
     wait(*g2[1], *g2[2])
     smooth_rows(0, 0)
     smooth_rows(lead - 1, 0)

time: 86.5 us -> 86.1 us (level)
  no operation moved by 1% of the time
where the time goes in v6:
time: 86.1 us
  Pallas kernels  85.4 us (99%)
    pallas_call x1, Pallas kernels, body(): pl.pallas_call(kernel, name='design_iteration', out_shape=[jax.ShapeDtype...  82.1 us
    pallas_call x1, Pallas kernels, body(): pl.pallas_call(last_kernel, name='last_filter', out_shape=[jax.ShapeDtype...  3.32 us

profile of v6, /device:TPU:129, one launch (start us, length us, event | category | flops | bytes accessed | tf_op | source)
XLA Modules:
  0.0 86.1 jit_solution(10409699151394180955)
XLA Ops:
  0.6 82.1 %design_iteration.1 = (f32[16,64,256]{2,1,0:T(8,128)}, f32[16,64,256]{2,1,0:T(8,128)}, f32[4,16,16,256]{3,2,1,0:T(8,128)}) custom-call(f32[16,16,1024]{2,1,0:T(8,128)} %mat_h.1, s32[16,64,256]{2,1,0:T(8,128)} %mark_h.1, f32[16,64,256]{2,1,0:T(8,128)} %press_h.1, f32[16,64,256]{2,1,0:T(8,128)} %warm_h.1, f32[16,64,256]{2,1,0:T(8,128)} %vel_h.1, ...), custom_call_target="tpu_custom_call" | custom-call | tf_op jit(solution)/shard_map/design_iteration/pallas_call | solution.py:480
  82.7 3.3 %last_filter.1 = (f32[16,64,256]{2,1,0:T(8,128)}, f32[16,64,256]{2,1,0:T(8,128)}, f32[16,16,1024]{2,1,0:T(8,128)}) custom-call(f32[16,64,256]{2,1,0:T(8,128)} %get-tuple-element.6.speed_h, f32[16,64,256]{2,1,0:T(8,128)} %get-tuple-element.7.temper_h, f32[4,16,16,256]{3,2,1,0:T(8,128)} %get-tuple-element.8.slab_h), custom_call_target="tpu_custom_call" | custom-call | tf_op jit(solution)/shard_map/last_filter/pallas_call | solution.py:502
